TPU v7x, 32 devices: a whole 2x2x4 slice. The times are simulated.
32 devices in a mesh: stream: 8 (over z, x), tm: 4 (over y, core).
Axes of the slice: x: 2, y: 2, z: 4, core: 2. Of those that a mesh axis runs over, the one named last changes fastest.
Arguments:
- raw: bfloat16 [4096, 4096], P('stream', 'tm'), may hold values from -400 to 400
- taps: float32 [65], replicated, may hold values from -0.75 to 0.75
Outputs:
- information: float32 [9, 4096, 4096], P(None, 'stream', 'tm')
- filtered: bfloat16 [4096, 4096], P('stream', 'tm')
All inputs are finite; a program needn't handle non-finite values.
Results may differ from a plain program's by a relative error of at most 0.0014.
Values may be sent and summed in bfloat16 or wider, within the bound.
A program may use at most 320 MiB of HBM per device.

v0:
```python
import jax
import jax.numpy as jnp
from jax import lax
from jax.sharding import PartitionSpec as P

LAGS = 9
REACH = 4


def padded(shard, sides, width):
    for axis, dim in sides:
        peers, length = (lax.axis_size(axis), shard.shape[dim])
        up = [(i, (i + 1) % peers) for i in range(peers - 1)]
        down = [(j, i) for i, j in up]
        last = lax.slice_in_dim(shard, length - width, length, axis=dim)
        initial = lax.slice_in_dim(shard, 0, width, axis=dim)
        before = lax.ppermute(last, axis, up)
        after = lax.ppermute(initial, axis, down)
        shard = jnp.concatenate([before, shard, after], axis=dim)
    return shard


def apply_filter(block, taps):
    kernel = taps.reshape(1, 1, -1)
    signal = block.astype(jnp.float32)[:, None, :]
    return lax.conv_general_dilated(signal, kernel, (1,), "VALID", precision=lax.Precision.HIGHEST)[
        :, 0, :
    ]


def shards(raw, taps):
    rows, bins = raw.shape
    streams = rows * lax.axis_size("stream")
    tm_count = lax.axis_size("tm")
    tm_place = lax.axis_index("tm")
    stream_place = lax.axis_index("stream")
    half = (taps.shape[0] - 1) // 2
    wide = padded(raw, (("tm", 1),), half)
    filtered = apply_filter(wide, taps).astype(jnp.bfloat16)
    extended = padded(filtered, (("tm", 1),), REACH)
    start_totals = jnp.zeros((LAGS, rows, streams), jnp.float32)
    start_energy = jnp.zeros((streams,), jnp.float32)
    start = jnp.int32(0)
    totals = start_totals
    energy = start_energy
    piece = jax.tree.map(lambda part: lax.all_gather(part, "stream", axis=0, tiled=True), extended)
    shifted = jnp.stack([piece[:, lag : lag + bins] for lag in range(LAGS)], 0)
    moments = jnp.einsum("it,ljt->lij", filtered, shifted, preferred_element_type=jnp.float32)
    core = piece[:, REACH : REACH + bins].astype(jnp.float32)
    moments, block_energy = (moments, jnp.sum(core * core, axis=1))
    totals = lax.dynamic_update_slice(totals, moments, (jnp.int32(0), jnp.int32(0), start))
    energy = lax.dynamic_update_slice(energy, block_energy, (start,))
    totals, energy = (totals, energy)
    moments = lax.psum_scatter(totals, "tm", scatter_dimension=2, tiled=True)
    energy = lax.psum(energy, "tm")
    columns = streams // tm_count
    row_energy = lax.dynamic_slice_in_dim(energy, stream_place * rows, rows, 0)
    column_energy = lax.dynamic_slice_in_dim(energy, tm_place * columns, columns, 0)
    norms = 1.25 * jnp.sqrt((row_energy[:, None] + 1e-05) * (column_energy[None, :] + 1e-05))
    ratio = moments / norms[None, :, :]
    information = -0.5 * jnp.log(1.0 - ratio * ratio)
    return (information, filtered)


def solution(mesh):
    placed = (P("stream", "tm"), P())
    return jax.shard_map(
        shards,
        mesh=mesh,
        in_specs=placed,
        out_specs=(P(None, "stream", "tm"), P("stream", "tm")),
        check_vma=False,
    )
```

profile of v0, /device:TPU:0, one launch (start us, length us, event | category | flops | bytes accessed | tf_op | source)
XLA Modules:
  0.0 1039.2 jit_solution(15116787475060685442)
XLA Ops:
  7.2 1.5 copy.12
  8.7 2.4 collective-permute-start
  11.1 1.3 collective-permute-start.1
  12.4 0.8 copy.16
  13.2 3.2 collective-permute-done.1
  16.3 0.1 maximum_bitcast_fusion
  16.4 156.2 %convolution_convert_fusion = bf16[512,1,1024]{0,1,2:T(2,128)(2,1)S(1)} fusion(f32[1,1,65]{1,0,2:T(1,128)S(1)} %copy.16, bf16[512,1,1088]{0,2,1:T(8,128)(2,1)S(1)} %maximum_bitcast_fusion), kind=kOutput, calls=%fused_computation.20 | convolution fusion | flops 409468928 | bytes 2162948 | tf_op jit(solution)/shard_map/conv_general_dilated | solution.py:26
  172.6 2.6 copy.17
  175.2 0.1 fusion.10
  175.3 4.5 collective-permute-start.2
  179.9 1.3 collective-permute-start.3
  181.2 1.9 collective-permute-done.3
  183.1 2.4 concatenate.7
  185.5 0.0 reduce-scatter.2.cloned.1.call-start
  185.6 141.2 %all-gather.2.cloned.1.call-done = bf16[4096,1032]{1,0:T(8,128)(2,1)} async-done(((bf16[512,1032]{1,0:T(8,128)(2,1)}), bf16[4096,1032]{1,0:T(8,128)(2,1)}) %all-gather.2.cloned.1.call-update) | async-done | bytes 8454160 | tf_op jit(solution)/shard_map/all_gather | solution.py:46
  326.8 7.7 fusion.7
  334.4 12.1 %fusion.6 = bf16[9,4096,1024]{2,1,0:T(8,128)(2,1)} fusion(bf16[9,4096,1024]{2,1,0:T(8,128)(2,1)} %fusion.7, bf16[4096,1032]{1,0:T(8,128)(2,1)} %all-gather.2.cloned.1.call-done), kind=kLoop, calls=%fused_computation.16 | loop fusion | bytes 16777216
  346.5 12.2 %fusion.5 = bf16[9,4096,1024]{2,1,0:T(8,128)(2,1)} fusion(bf16[9,4096,1024]{2,1,0:T(8,128)(2,1)} %fusion.6, bf16[4096,1032]{1,0:T(8,128)(2,1)} %all-gather.2.cloned.1.call-done), kind=kLoop, calls=%fused_computation.14 | loop fusion | bytes 16777216
  358.7 12.4 %fusion.4 = bf16[9,4096,1024]{2,1,0:T(8,128)(2,1)} fusion(bf16[9,4096,1024]{2,1,0:T(8,128)(2,1)} %fusion.5, bf16[4096,1032]{1,0:T(8,128)(2,1)} %all-gather.2.cloned.1.call-done), kind=kLoop, calls=%fused_computation.12 | loop fusion | bytes 16777216
  371.1 12.1 %bitcast_dynamic-update-slice_fusion = bf16[9,4096,1024]{2,1,0:T(8,128)(2,1)} fusion(bf16[9,4096,1024]{2,1,0:T(8,128)(2,1)} %fusion.4, bf16[4096,1032]{1,0:T(8,128)(2,1)} %all-gather.2.cloned.1.call-done), kind=kLoop, calls=%fused_computation.19 | loop fusion | bytes 16777216
  383.2 12.4 %fusion.3 = bf16[9,4096,1024]{2,1,0:T(8,128)(2,1)} fusion(bf16[9,4096,1024]{2,1,0:T(8,128)(2,1)} %bitcast_dynamic-update-slice_fusion, bf16[4096,1032]{1,0:T(8,128)(2,1)} %all-gather.2.cloned.1.call-done), kind=kLoop, calls=%fused_computation.10 | loop fusion | bytes 16777216
  395.6 12.1 %fusion.2 = bf16[9,4096,1024]{2,1,0:T(8,128)(2,1)} fusion(bf16[9,4096,1024]{2,1,0:T(8,128)(2,1)} %fusion.3, bf16[4096,1032]{1,0:T(8,128)(2,1)} %all-gather.2.cloned.1.call-done), kind=kLoop, calls=%fused_computation.8 | loop fusion | bytes 16777216
  407.8 12.1 %fusion.1 = bf16[9,4096,1024]{2,1,0:T(8,128)(2,1)} fusion(bf16[9,4096,1024]{2,1,0:T(8,128)(2,1)} %fusion.2, bf16[4096,1032]{1,0:T(8,128)(2,1)} %all-gather.2.cloned.1.call-done), kind=kLoop, calls=%fused_computation.6 | loop fusion | bytes 16777216
  419.9 12.5 %fusion = bf16[9,4096,1024]{2,1,0:T(8,128)(2,1)} fusion(bf16[9,4096,1024]{2,1,0:T(8,128)(2,1)} %fusion.1, bf16[4096,1032]{1,0:T(8,128)(2,1)} %all-gather.2.cloned.1.call-done), kind=kLoop, calls=%fused_computation.4 | loop fusion | bytes 16777216 | tf_op jit(solution)/shard_map/stack | solution.py:47
  432.4 61.2 %convolution_bitcast_fusion = f32[9,512,4096]{1,2,0:T(8,128)} fusion(bf16[9,4096,1024]{2,1,0:T(8,128)(2,1)} %fusion, bf16[512,1,1024]{2,0,1:T(8,128)(2,1)S(1)} %copy.17), kind=kOutput, calls=%fused_computation | convolution fusion | flops 38654705664 | bytes 152043520 | tf_op jit(solution)/shard_map/it,ljt->lij/dot_general | solution.py:48
  493.7 11.5 %multiply_reduce_fusion = f32[4096]{0:T(1024)S(1)} fusion(bf16[4096,1032]{1,0:T(8,128)(2,1)} %all-gather.2.cloned.1.call-done), kind=kLoop, calls=%fused_computation.2 | loop fusion | flops 12578816 | bytes 8404992 | tf_op jit(solution)/shard_map/reduce_sum | solution.py:50
  505.2 10.5 %psum.7 = f32[4096]{0:T(1024)S(1)} all-reduce(f32[4096]{0:T(1024)S(1)} %multiply_reduce_fusion), channel_id=1, replica_groups=mesh['stream'=8,'tm'=4] {'tm'}, use_global_device_ids=true, to_apply=%region_2.0 | all-reduce | flops 4096 | bytes 32768 | tf_op jit(solution)/shard_map/psum | solution.py:55
  515.6 0.1 dynamic-slice_add_fusion.1
  515.7 0.7 sqrt_multiply_fusion
  516.4 481.3 %reduce-scatter.2.cloned.1.call-done = f32[9,512,1024]{1,2,0:T(8,128)} async-done(((f32[9,512,4096]{1,2,0:T(8,128)}), f32[9,512,1024]{1,2,0:T(8,128)}) %reduce-scatter.2.cloned.1.call-update) | async-done | bytes 18874384 | tf_op jit(solution)/shard_map/reduce_scatter | solution.py:54
  997.7 15.8 %log_multiply_fusion = f32[9,512,1024]{1,2,0:T(8,128)} fusion(f32[9,512,1024]{1,2,0:T(8,128)} %reduce-scatter.2.cloned.1.call-done, f32[512,1024]{0,1:T(8,128)S(1)} %sqrt_multiply_fusion), kind=kLoop, calls=%fused_computation.1 | loop fusion | flops 18874368 | bytes 39845888 | tf_op jit(solution)/shard_map/mul | solution.py:61
  1013.5 18.6 %copy.18 = f32[9,512,1024]{2,1,0:T(8,128)} copy(f32[9,512,1024]{1,2,0:T(8,128)} %log_multiply_fusion) | data formatting | bytes 37748736
  (9 shorter events, 0.1 us)
Async XLA Ops:
  7.2 319.6 %all-gather.2.cloned.1.call-start = ((), (), s32[]{:S(2)}) async-start(), calls=%async_computation.1 | async-start | bytes 10616832 | tf_op jit(solution)/shard_map/all_gather | solution.py:46
  8.7 4.4 collective-permute-start
  11.1 5.2 collective-permute-start.1
  175.2 257.2 %copy-start = (bf16[512,1,1024]{2,0,1:T(8,128)(2,1)}, bf16[512,1,1024]{2,0,1:T(8,128)(2,1)S(1)}, u32[]{:S(2)}) copy-start(bf16[512,1,1024]{2,0,1:T(8,128)(2,1)S(1)} %copy.17) | copy-start | bytes 3145732
  175.3 5.9 collective-permute-start.2
  179.9 3.2 collective-permute-start.3
  185.5 812.1 %reduce-scatter.2.cloned.1.call-start = ((), (), s32[]{:S(2)}) async-start(), calls=%async_computation.2 | async-start | bytes 94371840 | tf_op jit(solution)/shard_map/reduce_scatter | solution.py:54
Sparse Core Ops, SparseCore 0:
  185.7 141.0 all-gather.1
  493.8 503.8 reduce-scatter.1
where the time goes:
time: 1060 us; the launch traced here: 1040 us
  waiting for transfers between devices  628 us (59%)
  matrix products  217 us (20%)
  local copies, waits for them, and re-layouts  132 us (12%)
  other arithmetic  28.1 us (3%)
  between operations  14.3 us (1%)
    reduce_scatter x1, waiting for transfers between devices, shards(): moments = lax.psum_scatter(totals, 'tm', scatter_dimension=2, tiled=True)  481 us
    conv_general_dilated x1, matrix products, apply_filter(): lax.conv_general_dilated(signal, kernel, (1,), 'VALID', precision=lax.Pre...  156 us
    all_gather x1, waiting for transfers between devices, shards(): lax.all_gather(part, 'stream', axis=0, tiled=True)  141 us
    unnamed x12, local copies, waits for them, and re-layouts  113 us
    dot_general x1, matrix products, shards(): jnp.einsum('it,ljt->lij', filtered, shifted, preferred_element_type=jnp.f...  61.2 us
  transfers between devices with their start and end apart: 6, of which 4 were waited for; matrix products, arithmetic and copies ran while one was open for 1% of the time, Pallas kernels for 0%

commit v1 on v0

v1 whole, which is shorter than its diff:
```python
import functools

import jax
import jax.numpy as jnp
from jax import lax
from jax.experimental import pallas as pl
from jax.experimental.pallas import tpu as pltpu
from jax.sharding import PartitionSpec as P

LAGS = 9
REACH = 4
PAD = 128
OUT = 256
WIN = OUT + 2 * PAD
CHUNK = 32
NT = (((1,), (1,)), ((), ()))
MESH = pl.DeviceIdType.MESH


def gather_kernel(streams, blocks, raw_ref, base_ref, a_ref, b_ref, full, bands, *sems):
    p1_send, p1_recv, up_send, down_send, z_recv, x_send, x_recv = sems
    rows, width = raw_ref.shape
    time = a_ref.shape[1]
    layers = streams // blocks
    chunks = rows // CHUNK
    s = lax.axis_index("stream")
    t = lax.axis_index("tm")
    z = s // blocks
    g = s % blocks
    source = z == t

    barrier = pltpu.get_barrier_semaphore()

    def greet(target):
        pl.semaphore_signal(barrier, inc=1, device_id=target, device_id_type=MESH)

    def peer_tm(d):
        return (t + d) % 4

    def peer_g(d):
        return z * blocks + (g + d) % blocks

    for d in (1, 2, 3):
        greet({"tm": peer_tm(d)})
    for d in range(1, blocks):
        greet({"stream": peer_g(d)})

    @pl.when(z > 0)
    def _():
        greet({"stream": s - blocks})

    @pl.when(z < layers - 1)
    def _():
        greet({"stream": s + blocks})

    count = 3 + blocks - 1 + jnp.where(z > 0, 1, 0) + jnp.where(z < layers - 1, 1, 0)
    pl.semaphore_wait(barrier, count)

    def raw_rows(c):
        return pl.ds(pl.multiple_of(c * CHUNK, CHUNK), CHUNK)

    def lanes_of(q):
        return pl.ds(pl.multiple_of(PAD + q * width, PAD), width)

    def p1_copy(c, d):
        return pltpu.make_async_remote_copy(
            src_ref=raw_ref.at[raw_rows(c)],
            dst_ref=full.at[raw_rows(c), lanes_of(t)],
            send_sem=p1_send.at[d - 1, c],
            recv_sem=p1_recv.at[d - 1, c],
            device_id={"tm": peer_tm(d)},
            device_id_type=MESH,
        )

    @pl.loop(0, chunks)
    def _(c):
        for d in (2, 3, 1):
            p1_copy(c, d).start()

    full[:, lanes_of(t)] = raw_ref[...]
    full[:, :PAD] = jnp.zeros((rows, PAD), full.dtype)
    full[:, PAD + time:] = jnp.zeros((rows, PAD), full.dtype)
    band = pltpu.roll(jnp.broadcast_to(base_ref[...], (OUT, WIN)), 0, 1, stride=1, stride_axis=0)
    for k in range(3):
        part = band.astype(jnp.bfloat16)
        bands[k] = part
        band = band - part.astype(jnp.float32)

    def b_rows(c, q):
        return pl.ds(pl.multiple_of(q * rows + c * CHUNK, CHUNK), CHUNK)

    def z_copy(c, step, send):
        return pltpu.make_async_remote_copy(
            src_ref=b_ref.at[b_rows(c, g)],
            dst_ref=b_ref.at[b_rows(c, g)],
            send_sem=send.at[c],
            recv_sem=z_recv.at[c],
            device_id={"stream": s + step},
            device_id_type=MESH,
        )

    def x_copy(c, d):
        return pltpu.make_async_remote_copy(
            src_ref=b_ref.at[b_rows(c, g)],
            dst_ref=b_ref.at[b_rows(c, g)],
            send_sem=x_send.at[d - 1, c],
            recv_sem=x_recv.at[d - 1, c],
            device_id={"stream": peer_g(d)},
            device_id_type=MESH,
        )

    rising = (z >= t) & (z < layers - 1)
    falling = (z <= t) & (z > 0)

    def forward(c):
        @pl.when(rising)
        def _():
            z_copy(c, blocks, up_send).start()

        @pl.when(falling)
        def _():
            z_copy(c, -blocks, down_send).start()

        for d in range(1, blocks):
            x_copy(c, d).start()

    @pl.loop(0, chunks)
    def _(c):
        @pl.when(jnp.logical_not(source))
        def _():
            z_copy(c, jnp.where(z > t, -blocks, blocks), up_send).wait_recv()
            forward(c)

        for d in (2, 3, 1):
            p1_copy(c, d).wait_recv()
        here = raw_rows(c)
        stack = jnp.concatenate(
            [full[here, OUT * b:OUT * b + WIN] for b in range(time // OUT)], axis=0
        )
        total = lax.dot_general(stack, bands[2], NT, preferred_element_type=jnp.float32)
        total += lax.dot_general(stack, bands[1], NT, preferred_element_type=jnp.float32)
        total += lax.dot_general(stack, bands[0], NT, preferred_element_type=jnp.float32)
        values = total.astype(jnp.bfloat16)
        for b in range(time // OUT):
            a_ref[here, OUT * b:OUT * (b + 1)] = values[CHUNK * b:CHUNK * (b + 1)]

        @pl.when(source)
        def _():
            there = b_rows(c, g)
            for b in range(time // OUT):
                b_ref[there, OUT * b:OUT * (b + 1)] = values[CHUNK * b:CHUNK * (b + 1)]
            forward(c)

    @pl.loop(0, chunks)
    def _(c):
        for d in range(1, blocks):
            x_copy(c, d).wait_recv()

    @pl.loop(0, chunks)
    def _(c):
        for d in (1, 2, 3):
            p1_copy(c, d).wait_send()
        for d in range(1, blocks):
            x_copy(c, d).wait_send()

        @pl.when(rising)
        def _():
            z_copy(c, blocks, up_send).wait_send()

        @pl.when(falling)
        def _():
            z_copy(c, -blocks, down_send).wait_send()


def gather(raw, base, streams, blocks):
    rows, width = raw.shape
    time = width * 4
    chunks = rows // CHUNK
    dma = pltpu.SemaphoreType.DMA
    vmem = pl.BlockSpec(memory_space=pltpu.VMEM)
    return pl.pallas_call(
        functools.partial(gather_kernel, streams, blocks),
        out_shape=(
            jax.ShapeDtypeStruct((rows, time), jnp.bfloat16),
            jax.ShapeDtypeStruct((rows * blocks, time), jnp.bfloat16),
        ),
        in_specs=[vmem, vmem],
        out_specs=(vmem, vmem),
        scratch_shapes=[
            pltpu.VMEM((rows, time + 2 * PAD), jnp.bfloat16),
            pltpu.VMEM((3, OUT, WIN), jnp.bfloat16),
            dma((3, chunks)),
            dma((3, chunks)),
            dma((chunks,)),
            dma((chunks,)),
            dma((chunks,)),
            dma((max(blocks - 1, 1), chunks)),
            dma((max(blocks - 1, 1), chunks)),
        ],
        compiler_params=pltpu.CompilerParams(
            collective_id=0, has_side_effects=True, vmem_limit_bytes=40 * 1024 * 1024
        ),
        cost_estimate=pl.CostEstimate(
            flops=6 * rows * time * WIN, bytes_accessed=2 * rows * time * 8, transcendentals=0
        ),
    )(raw, base)


def inverse_norm(values):
    wide = values.astype(jnp.float32)
    energy = jnp.sum(wide * wide, axis=1, keepdims=True)
    return 1.0 / jnp.sqrt(1.25 * (energy + 1e-05))


def lag_kernel(a_ref, b_ref, out_ref, moved, row_norm, column_norm):
    lag = pl.program_id(0)
    j = pl.program_id(1)
    rows, time = a_ref.shape
    tile = out_ref.shape[2]
    step = 64

    @pl.when((lag == 0) & (j == 0))
    def _():
        @pl.loop(0, rows // step)
        def _(r):
            here = pl.ds(pl.multiple_of(r * step, step), step)
            row_norm[here] = jnp.broadcast_to(inverse_norm(a_ref[here]), (step, 128))

    @pl.when(lag == 0)
    def _():
        for r in range(tile // 128):
            here = pl.ds(pl.multiple_of(j * tile + r * 128, 128), 128)
            column = jnp.broadcast_to(inverse_norm(b_ref[here]), (128, 128))
            column_norm[:, here] = jnp.transpose(column)[:8]

    for k in range(LAGS):
        @pl.when((lag == k) & (j == 0))
        def _():
            shift = k - REACH

            @pl.loop(0, rows // 32)
            def _(r):
                here = pl.ds(pl.multiple_of(r * 32, 32), 32)
                if shift == 0:
                    moved[here] = a_ref[here]
                else:
                    wide = a_ref[here].astype(jnp.float32)
                    turned = pltpu.roll(wide, shift % time, 1)
                    place = lax.broadcasted_iota(jnp.int32, turned.shape, 1) - shift
                    kept = (place >= 0) & (place < time)
                    moved[here] = jnp.where(kept, turned, 0.0).astype(jnp.bfloat16)

    there = pl.ds(pl.multiple_of(j * tile, tile), tile)
    moments = lax.dot_general(moved[...], b_ref[there], NT, preferred_element_type=jnp.float32)
    ratio = moments * row_norm[:, :1] * column_norm[:1, there]
    out_ref[0] = -0.5 * jnp.log(1.0 - ratio * ratio)


def lagged(a, b):
    rows, time = a.shape
    columns = b.shape[0]
    tile = 256
    return pl.pallas_call(
        lag_kernel,
        out_shape=jax.ShapeDtypeStruct((LAGS, rows, columns), jnp.float32),
        grid=(LAGS, columns // tile),
        in_specs=[pl.BlockSpec(memory_space=pltpu.VMEM), pl.BlockSpec(memory_space=pltpu.VMEM)],
        out_specs=pl.BlockSpec((1, rows, tile), lambda lag, j: (lag, 0, j)),
        scratch_shapes=[
            pltpu.VMEM((rows, time), jnp.bfloat16),
            pltpu.VMEM((rows, 128), jnp.float32),
            pltpu.VMEM((8, columns), jnp.float32),
        ],
        compiler_params=pltpu.CompilerParams(vmem_limit_bytes=48 * 1024 * 1024),
        cost_estimate=pl.CostEstimate(
            flops=2 * LAGS * rows * columns * time,
            bytes_accessed=4 * LAGS * rows * columns,
            transcendentals=LAGS * rows * columns,
        ),
    )(a, b)


def shards(raw, taps):
    width = raw.shape[1]
    streams = lax.axis_size("stream")
    blocks = streams // lax.axis_size("tm")
    half = (taps.shape[0] - 1) // 2
    lead = PAD - half
    base = jnp.pad(taps, (lead, WIN - lead - taps.shape[0]))[None, :]
    a, b = gather(raw, base, streams, blocks)
    filtered = lax.dynamic_slice_in_dim(a, lax.axis_index("tm") * width, width, 1)
    return (lagged(a, b), filtered)


def solution(mesh):
    placed = (P("stream", "tm"), P())
    return jax.shard_map(
        shards,
        mesh=mesh,
        in_specs=placed,
        out_specs=(P(None, "stream", "tm"), P("stream", "tm")),
        check_vma=False,
    )
```

time: 1060 us -> 202 us (0.19)
  the two profiles are of different devices: /device:TPU:0 before, /device:TPU:5 now
where the time goes in v1:
time: 202 us; the launch traced here: 201 us
  Pallas kernels  193 us (96%)
  local copies, waits for them, and re-layouts  7.43 us (4%)
    pallas_call x1, Pallas kernels, gather(): pl.pallas_call(functools.partial(gather_kernel, streams, blocks), out_sha...  116 us
    pallas_call x1, Pallas kernels, lagged(): pl.pallas_call(lag_kernel, out_shape=jax.ShapeDtypeStruct((LAGS, rows, co...  77.1 us
    unnamed x6, local copies, waits for them, and re-layouts  4.44 us

profile of v1, /device:TPU:5, one launch (start us, length us, event | category | flops | bytes accessed | tf_op | source)
XLA Modules:
  0.0 201.4 jit_solution(1783651405753581076)
XLA Ops:
  0.6 0.7 pad.4
  1.4 0.0 copy-start.1
  1.4 1.2 copy-done.1
  2.6 116.2 %shard_map.41 = (bf16[512,4096]{1,0:T(8,128)(2,1)S(1)}, bf16[1024,4096]{1,0:T(8,128)(2,1)S(1)}) custom-call(bf16[512,1024]{1,0:T(8,128)(2,1)S(1)} %copy-done.1, f32[1,512]{1,0:T(1,128)S(1)} %bitcast.1), custom_call_target="tpu_custom_call" | custom-call | flops 6442450944 | bytes 33554432 | tf_op jit(solution)/shard_map/pallas_call | solution.py:181
  118.8 0.0 copy-start.2
  118.8 3.2 %copy-done.2 = bf16[1024,4096]{1,0:T(8,128)(2,1)} copy-done((bf16[1024,4096]{1,0:T(8,128)(2,1)}, bf16[1024,4096]{1,0:T(8,128)(2,1)S(1)}, u32[]{:S(2)}) %copy-start.2) | copy-done | bytes 8388632
  122.0 0.0 copy-start
  122.0 77.1 %shard_map.42 = f32[9,512,1024]{2,1,0:T(8,128)} custom-call(bf16[512,4096]{1,0:T(8,128)(2,1)S(1)} %get-tuple-element.4.a_ref, bf16[1024,4096]{1,0:T(8,128)(2,1)} %copy-done.2), custom_call_target="tpu_custom_call" | custom-call | flops 38654705664 | bytes 18874368 | tf_op jit(solution)/shard_map/pallas_call | solution.py:263
  199.1 0.0 copy-done
  199.1 2.3 %constant_dynamic-slice_fusion = bf16[512,1024]{1,0:T(8,128)(2,1)} fusion(bf16[512,4096]{1,0:T(8,128)(2,1)} %copy-done, s32[]{:T(128)S(6)} %select_n.3), kind=kLoop, calls=%fused_computation | loop fusion | bytes 2097156 | tf_op jit(solution)/shard_map/dynamic_slice | solution.py:291
Async XLA Ops:
  1.4 1.2 copy-start.1
  118.8 3.2 %copy-start.2 = (bf16[1024,4096]{1,0:T(8,128)(2,1)}, bf16[1024,4096]{1,0:T(8,128)(2,1)S(1)}, u32[]{:S(2)}) copy-start(bf16[1024,4096]{1,0:T(8,128)(2,1)S(1)} %get-tuple-element.5.b_ref) | copy-start | bytes 25165828
  122.0 77.1 %copy-start = (bf16[512,4096]{1,0:T(8,128)(2,1)}, bf16[512,4096]{1,0:T(8,128)(2,1)S(1)}, u32[]{:S(2)}) copy-start(bf16[512,4096]{1,0:T(8,128)(2,1)S(1)} %get-tuple-element.4.a_ref) | copy-start | bytes 12582916
